TPU v7x, 512 devices: a whole 4x8x8 slice. The times are simulated.
512 devices in a mesh: seq: 16 (over z, x_hi), dp: 32 (over y, x_lo, core).
Axes of the slice: x: 4 (x_hi: 2, x_lo: 2; x = x_hi * 2 + x_lo), y: 8, z: 8, core: 2. Of those that a mesh axis runs over, the one named last changes fastest.
Arguments:
- inputs: bfloat16 [32, 2048, 4096], P('dp', 'seq'), may hold values from -6 to 6
- weights: bfloat16 [4096, 768], P(('seq', 'dp')), may hold values from -0.09375 to 0.09375
- lengths: int32 [32, 8], P('dp'), may hold values from 1 to 1024, 2048 in all within a row
- cotangent: bfloat16 [32, 2048, 256], P('dp', 'seq'), may hold values from -6 to 6
Outputs:
- normed: bfloat16 [32, 2048, 256], P('dp', 'seq')
- grad_inputs: bfloat16 [32, 2048, 4096], P('dp', 'seq')
- grad_weights: bfloat16 [4096, 768], P(('seq', 'dp'))
Inputs may be any that keep to these rules, and one draw needn't show every extreme that they name: Row b holds the lengths of the 8 documents packed end to end into sequence b; they sum to 2048.
All inputs are finite; a program needn't handle non-finite values.
Results may differ from a plain program's by a relative error of at most 0.03.
Values may be sent and summed in bfloat16 or wider, within the bound.
A program may use at most 64 MiB of HBM per device.

v0:
```python
import math

import jax
import jax.numpy as jnp
from jax import lax
from jax.sharding import PartitionSpec as P

HEADS = 2


epsilon = 1.0
highest = lax.Precision.HIGHEST


def carried_in(part, axis, combine, identity, reverse):
    count = lax.axis_size(axis)
    place = lax.axis_index(axis)
    ahead = count - 1 - place if reverse else place
    gathered = jax.tree.map(lambda a: lax.all_gather(a, axis), part)
    state = jax.tree.map(lambda a, e: jnp.zeros_like(a) + jnp.asarray(e, a.dtype), part, identity)

    def one(turn, state):
        source = count - 1 - turn if reverse else turn
        return combine(
            state, jax.tree.map(lambda a: lax.dynamic_index_in_dim(a, source, 0, False), gathered)
        )

    return lax.fori_loop(0, ahead, one, state)


def chain_combine(earlier, later):
    return (
        jnp.where(later[1] > 0, later[0], earlier[0] + later[0]),
        jnp.maximum(earlier[1], later[1]),
    )


def shards(inputs, weights, lengths, cotangent):
    tokens = inputs[0]
    rows = tokens.shape[0]
    width = tokens.shape[1]
    span = weights.shape[1] // 3
    head = span // HEADS
    shrink = 1.0 / head
    shard = lax.axis_index("seq")
    base = shard * rows
    offsets = jnp.arange(rows, dtype=jnp.int32)
    lengths_row = lengths[0]
    ends = jnp.cumsum(lengths_row)
    starts = ends - lengths_row

    def document(positions):
        return jnp.sum((starts[None, :] <= positions[:, None]).astype(jnp.int32), axis=1) - 1

    def split_heads(block):
        return block.reshape(block.shape[0], HEADS, head)

    docs = document(base + offsets)
    previous_doc = document(jnp.reshape(base - 1, (1,)))[0]
    leading = docs == previous_doc
    trailing = docs == docs[rows - 1]
    reset = jnp.any((starts >= base) & (starts < base + rows)).astype(jnp.float32).reshape(1, 1, 1)
    linked = (docs[:, None] == docs[None, :]) & (offsets[None, :] <= offsets[:, None])
    piece = lax.all_gather(weights, ("seq", "dp"), axis=0, tiled=True)
    running = jnp.dot(tokens, piece, preferred_element_type=jnp.float32)
    projected = running
    projected = projected.astype(jnp.bfloat16)
    query_flat = projected[:, :span]
    keys_flat = projected[:, span : 2 * span]
    values_flat = projected[:, 2 * span :]
    query = split_heads(query_flat)
    keys = split_heads(keys_flat)
    values = split_heads(values_flat)
    scores = jnp.where(
        linked[None],
        shrink * jnp.einsum("thd,jhd->htj", query, keys, preferred_element_type=jnp.float32),
        0.0,
    )
    attended = jnp.einsum("htj,jhd->thd", scores, values.astype(jnp.float32), precision=highest)
    neutral = (jnp.zeros((HEADS, head, head), jnp.float32), jnp.zeros((1, 1, 1), jnp.float32))
    tail_keys = jnp.where(trailing[:, None, None], keys, jnp.zeros_like(keys))
    local_state = jnp.einsum("thd,the->hde", tail_keys, values, preferred_element_type=jnp.float32)
    incoming, unused = carried_in((local_state, reset), "seq", chain_combine, neutral, False)
    attended = attended + jnp.where(
        leading[:, None, None],
        shrink * jnp.einsum("thd,hde->the", query.astype(jnp.float32), incoming, precision=highest),
        0.0,
    )
    inverse = lax.rsqrt(jnp.mean(attended * attended, axis=2, keepdims=True) + epsilon)
    normed = (attended * inverse).astype(jnp.bfloat16)
    upstream = split_heads(cotangent[0]).astype(jnp.float32)
    along = jnp.mean(upstream * attended, axis=2, keepdims=True)
    grad_attended = (inverse * upstream - attended * inverse * inverse * inverse * along).astype(
        jnp.bfloat16
    )
    mixed = jnp.where(
        linked[None],
        shrink
        * jnp.einsum("the,jhe->htj", grad_attended, values, preferred_element_type=jnp.float32),
        0.0,
    )
    grad_query = jnp.einsum("htj,jhd->thd", mixed, keys.astype(jnp.float32), precision=highest)
    grad_keys = jnp.einsum("htj,thd->jhd", mixed, query.astype(jnp.float32), precision=highest)
    grad_values = jnp.einsum(
        "htj,the->jhe", scores, grad_attended.astype(jnp.float32), precision=highest
    )
    grad_query = grad_query + jnp.where(
        leading[:, None, None],
        shrink
        * jnp.einsum(
            "the,hde->thd", grad_attended.astype(jnp.float32), incoming, precision=highest
        ),
        0.0,
    )
    head_query = jnp.where(leading[:, None, None], query, jnp.zeros_like(query))
    local_sums = jnp.einsum(
        "thd,the->hde", head_query, grad_attended, preferred_element_type=jnp.float32
    )
    arriving, unused = carried_in((local_sums, reset), "seq", chain_combine, neutral, True)
    grad_keys = grad_keys + jnp.where(
        trailing[:, None, None],
        shrink
        * jnp.einsum("the,hde->thd", values.astype(jnp.float32), arriving, precision=highest),
        0.0,
    )
    grad_values = grad_values + jnp.where(
        trailing[:, None, None],
        shrink * jnp.einsum("thd,hde->the", keys.astype(jnp.float32), arriving, precision=highest),
        0.0,
    )
    grad_all = jnp.concatenate(
        [
            grad_query.reshape(rows, span),
            grad_keys.reshape(rows, span),
            grad_values.reshape(rows, span),
        ],
        axis=1,
    ).astype(jnp.bfloat16)
    grad_inputs = lax.dot_general(
        grad_all, piece, (((1,), (1,)), ((), ())), preferred_element_type=jnp.float32
    ).astype(jnp.bfloat16)
    factor = 1.0 / math.sqrt(lax.axis_size("dp") * lax.axis_size("seq") * rows)
    columns = lax.all_to_all(tokens, "seq", split_axis=1, concat_axis=0, tiled=True)
    block = columns
    seq_sum = lax.dot_general(
        block,
        lax.all_gather(grad_all, "seq", axis=0, tiled=True),
        (((0,), (0,)), ((), ())),
        preferred_element_type=jnp.float32,
    )
    replica = (factor * seq_sum).astype(jnp.bfloat16)
    summed = lax.psum_scatter(
        replica.astype(jnp.float32).astype(jnp.bfloat16), "dp", scatter_dimension=0, tiled=True
    )
    return (normed.reshape(1, rows, span), grad_inputs.reshape(1, rows, width), summed)


def solution(mesh):
    placed = (P("dp", "seq", None), P(("seq", "dp"), None), P("dp", None), P("dp", "seq", None))
    return jax.shard_map(
        shards,
        mesh=mesh,
        in_specs=placed,
        out_specs=(P("dp", "seq", None), P("dp", "seq", None), P(("seq", "dp"), None)),
        check_vma=False,
    )
```

profile of v0, /device:TPU:1, one launch (start us, length us, event | category | flops | bytes accessed | tf_op | source)
XLA Modules:
  0.0 1308.1 jit_solution(5373159871846229061)
XLA Ops:
  7.2 0.7 all-gather.7.cloned.1.call-update
  8.0 0.8 reduce-window.4
  8.8 1.3 fusion.35
  11.4 0.7 broadcast_compare_fusion.1
  12.1 816.3 %all-gather.7.cloned.1.call-done = bf16[4096,768]{1,0:T(8,128)(2,1)} async-done(((bf16[8,768]{1,0:T(8,128)(2,1)}), bf16[4096,768]{1,0:T(8,128)(2,1)}) %all-gather.7.cloned.1.call-update) | async-done | bytes 6291472 | tf_op jit(solution)/shard_map/all_gather | solution.py:64
  828.4 4.1 convolution_convert_fusion.1
  832.6 0.8 fusion.19
  833.6 0.6 and_reduce_fusion
  834.8 1.2 dynamic-slice
  836.0 0.7 dynamic-update-slice
  836.7 32.9 %all-reduce = f32[16]{0:T(128)S(1)} all-reduce(f32[16]{0:T(128)S(1)} %dynamic-update-slice), channel_id=1, replica_groups=mesh['seq'=16,'dp'=32] {'seq'}, use_global_device_ids=true, to_apply=%add | all-reduce | flops 16 | bytes 128
  870.0 56.1 %all-gather.11.cloned.1.call-done = f32[32,128,128]{2,1,0:T(8,128)} async-done(((f32[2,128,128]{2,1,0:T(8,128)}), f32[32,128,128]{2,1,0:T(8,128)}) %all-gather.11.cloned.1.call-update) | async-done | bytes 2097168 | tf_op jit(solution)/shard_map/all_gather | solution.py:19
  926.8 0.8 fusion.21
  928.4 119.1 %all-gather.13.cloned.1.call-done = f32[32,128,128]{2,1,0:T(8,128)} async-done(((f32[2,128,128]{2,1,0:T(8,128)}), f32[32,128,128]{2,1,0:T(8,128)}) %all-gather.13.cloned.1.call-update) | async-done | bytes 2097168 | tf_op jit(solution)/shard_map/all_gather | solution.py:19
  1047.6 33.1 %while.27 = (s32[]{:T(128)}, f32[2,128,128]{2,1,0:T(8,128)S(1)}, s32[]{:T(128)}, f32[16,1,1,1]{0,3,2,1:T(1,128)S(1)}, f32[16,2,128,128]{3,2,1,0:T(8,128)}, /*index=5*/s32[]{:T(128)}, s32[]{:T(128)}, s32[]{:T(128)}, s32[]{:T(128)}) while((s32[]{:T(128)}, f32[2,128,128]{2,1,0:T(8,128)S(1)}, s32[]{:T(128)}, f32[16,1,1,1]{0,3,2,1:T(1,128)S(1)}, ...), condition=%wide.region_9.10_spmd, body=%wide.region_8.9_spmd.sunk | while | flops 65543 | bytes 393377 | solution.py:28
  1047.6 0.6 fusion.64
  1048.2 1.6 add_select_fusion.5
  1049.8 0.6 fusion.64
  1050.4 1.6 add_select_fusion.5
  1052.0 0.6 fusion.64
  1052.6 1.6 add_select_fusion.5
  1054.2 0.6 fusion.64
  1054.8 1.6 add_select_fusion.5
  1056.4 0.6 fusion.64
  1057.0 1.6 add_select_fusion.5
  1058.6 0.6 fusion.64
  1059.2 1.6 add_select_fusion.5
  1060.8 0.6 fusion.64
  1061.4 1.6 add_select_fusion.5
  1063.0 0.6 fusion.64
  1063.6 1.6 add_select_fusion.5
  1065.2 0.6 fusion.64
  1065.8 1.6 add_select_fusion.5
  1068.0 1.6 add_select_fusion.5
  1070.2 1.6 add_select_fusion.5
  1072.4 1.6 add_select_fusion.5
  1074.7 1.6 add_select_fusion.5
  1076.9 1.6 add_select_fusion.5
  1079.1 1.6 add_select_fusion.5
  1081.7 0.7 pad_maximum_fusion
  1082.4 0.7 copy.109
  1083.1 29.7 %all_to_all.19 = bf16[128,16,256]{0,2,1:T(8,128)(2,1)S(1)} all-to-all(bf16[128,16,256]{0,2,1:T(8,128)(2,1)S(1)} %bitcast.102), channel_id=1, replica_groups=mesh['seq'=16,'dp'=32] {'seq'}, dimensions={1} | all-to-all | bytes 2097152 | tf_op jit(solution)/shard_map/all_to_all | solution.py:143
  1113.4 69.7 %all-gather.9.cloned.1.call-done = bf16[2048,768]{0,1:T(8,128)(2,1)} async-done(((bf16[128,768]{0,1:T(8,128)(2,1)}), bf16[2048,768]{0,1:T(8,128)(2,1)}) %all-gather.9.cloned.1.call-update) | async-done | bytes 3145744 | tf_op jit(solution)/shard_map/all_gather | solution.py:147
  1183.1 2.9 fusion.2
  1185.9 0.9 copy.118
  1186.9 0.7 copy.111
  1187.6 5.9 fusion
  1193.6 108.0 %reduce-scatter.4.cloned.1.call-done = bf16[8,768]{1,0:T(8,128)(2,1)} async-done(((bf16[256,768]{1,0:T(8,128)(2,1)}), bf16[8,768]{1,0:T(8,128)(2,1)}) %reduce-scatter.4.cloned.1.call-update) | async-done | bytes 12304
  (47 shorter events, 8.0 us)
Async XLA Ops:
  7.2 821.2 %all-gather.7.cloned.1.call-start = ((), (), s32[]{:S(2)}) async-start(), calls=%async_computation.2 | async-start | bytes 6303744 | tf_op jit(solution)/shard_map/all_gather | solution.py:64
  7.9 918.2 %all-gather.11.cloned.1.call-start = ((), (), s32[]{:S(2)}) async-start(), calls=%async_computation.4 | async-start | bytes 2228224 | tf_op jit(solution)/shard_map/all_gather | solution.py:19
  12.1 821.4 %copy-start.1 = (bf16[1,128,256]{2,1,0:T(8,128)(2,1)S(1)}, bf16[1,128,256]{2,1,0:T(8,128)(2,1)}, u32[]{:S(2)}) copy-start(bf16[1,128,256]{2,1,0:T(8,128)(2,1)} %param.11) | copy-start | bytes 196612
  12.1 821.5 %copy-start.2 = (s32[1,8]{1,0:T(1,128)S(1)}, s32[1,8]{1,0:T(1,128)}, u32[]{:S(2)}) copy-start(s32[1,8]{1,0:T(1,128)} %param.10) | copy-start | bytes 100
  833.5 214.1 %all-gather.13.cloned.1.call-start = ((), (), s32[]{:S(2)}) async-start(), calls=%async_computation.5 | async-start | bytes 2228224 | tf_op jit(solution)/shard_map/all_gather | solution.py:19
  926.8 155.7 %copy-start = (bf16[1,128,4096]{2,1,0:T(8,128)(2,1)S(1)}, bf16[1,128,4096]{2,1,0:T(8,128)(2,1)}, u32[]{:S(2)}) copy-start(bf16[1,128,4096]{2,1,0:T(8,128)(2,1)} %param.8) | copy-start | bytes 3145732
  927.7 255.4 %all-gather.9.cloned.1.call-start = ((), (), s32[]{:S(2)}) async-start(), calls=%async_computation.3 | async-start | bytes 3342336 | tf_op jit(solution)/shard_map/all_gather | solution.py:147
  1082.4 219.2 %reduce-scatter.4.cloned.1.call-start = ((), (), s32[]{:S(2)}) async-start(), calls=%async_computation.6 | async-start | bytes 405504
Sparse Core Ops, SparseCore 0:
  10.2 818.0 all-gather.6
  833.6 92.5 all-gather.10
  929.9 117.6 all-gather.12
  1082.5 100.5 all-gather.8
  1187.0 114.5 reduce-scatter.3
where the time goes:
time: 1310 us
  waiting for transfers between devices  1170 us (89%)
  blocking collectives  62.6 us (5%)
  other arithmetic  37.1 us (3%)
  matrix products  17 us (1%)
  between operations  15.2 us (1%)
    all_gather x1, waiting for transfers between devices, shards(): piece = lax.all_gather(weights, ('seq', 'dp'), axis=0, tiled=True)  816 us
    all_gather x2, waiting for transfers between devices, carried_in(): gathered = jax.tree.map(lambda a: lax.all_gather(a, axis), part)  175 us
    unnamed x6, waiting for transfers between devices  109 us
    all_gather x1, waiting for transfers between devices, shards(): lax.all_gather(grad_all, 'seq', axis=0, tiled=True)  69.7 us
    unnamed x1, blocking collectives  32.9 us
    all_to_all x1, blocking collectives, shards(): lax.all_to_all(tokens, 'seq', split_axis=1, concat_axis=0, tiled=True)  29.7 us
  transfers between devices with their start and end apart: 5, of which 5 were waited for; matrix products, arithmetic and copies ran while one was open for 1% of the time, Pallas kernels for 0%

commit v1 on v0

v1 whole, which is shorter than its diff:
```python
import functools
import math

import jax
import jax.numpy as jnp
from jax import lax
from jax.experimental import pallas as pl
from jax.experimental.pallas import tpu as pltpu
from jax.sharding import PartitionSpec as P

HEAD = 128
NDOC = 8
ROWS = 16
MESH = pl.DeviceIdType.MESH
F32, BF16 = jnp.float32, jnp.bfloat16
ORDERS = (("x", "y", "z"), ("z", "x", "y"), ("y", "z", "x"))


def dot(a, b):
    return jnp.dot(a, b, preferred_element_type=F32)


def dot_nt(a, b):
    return lax.dot_general(a, b, (((1,), (1,)), ((), ())), preferred_element_type=F32)


def dot_tn(a, b):
    return lax.dot_general(a, b, (((0,), (0,)), ((), ())), preferred_element_type=F32)


def kernel(size, subs, tok, w, lens, cot, normed, gin, gw, *rest):
    (xsib, xt, wfull, wsend, wrecv, starts, csend, cots, proj, scan, keep, gbuf, mask, weak, hold, held, kept_n, nsend, nrecv,
     gown, gsend, grecv, dsend, drecv, send_sem, recv_sem) = rest[:26]
    wg, pg, ring, far, near = (rest[26 + 3 * i : 29 + 3 * i] for i in range(5))
    seqs = 2 * size["z"]
    rows = tok.shape[0]
    chunk = size["y"] * 2 * ROWS
    s, d = lax.axis_index("seq"), lax.axis_index("dp")
    c = lax.rem(d, 2)
    me = {"x": lax.rem(s, 2) * 2 + lax.rem(d // 2, 2), "y": d // 4, "z": s // 2}
    sibling = (s, d + 1 - 2 * c)

    def at(axis, place):
        spot = dict(me)
        spot[axis] = place
        return (spot["z"] * 2 + spot["x"] // 2, spot["y"] * 4 + lax.rem(spot["x"], 2) * 2 + c)

    def along(axis, step):
        return lax.rem(me[axis] + step + size[axis], size[axis])

    def remote(src, dst, index, target):
        return pltpu.make_async_remote_copy(
            src_ref=src,
            dst_ref=dst,
            send_sem=send_sem.at[index],
            recv_sem=recv_sem.at[index],
            device_id=target,
            device_id_type=MESH,
        )

    def drain(ref, sem):
        pltpu.make_async_copy(ref, ref, sem).wait()

    names = {}

    def number(*key):
        return names.setdefault(key, len(names))

    barrier = pltpu.get_barrier_semaphore()

    def greet(target):
        pl.semaphore_signal(barrier, inc=1, device_id=target, device_id_type=MESH)

    greet(sibling)
    for k in range(1, seqs):
        greet((lax.rem(s + k, seqs), d))
    for k in range(1, size["y"]):
        greet(at("y", along("y", k)))
    greet(at("x", along("x", 1)))
    greet(at("x", along("x", -1)))
    pl.semaphore_wait(barrier, 1 + seqs - 1 + size["y"] - 1 + 2)

    first = c == 0

    def head_columns(ref, part, mine):
        left = ref[:, part * 2 * HEAD : (2 * part + 1) * HEAD].astype(F32)
        right = ref[:, (2 * part + 1) * HEAD : (2 * part + 2) * HEAD].astype(F32)
        return jnp.where(first == mine, left, right)

    for p in range(3):
        wsend[:, p * HEAD : (p + 1) * HEAD] = head_columns(w, p, False)
    swap_w = remote(wsend, wrecv, number("w"), sibling)
    swap_w.start()
    swap_x = remote(tok, xsib, number("x"), sibling)
    swap_x.start()
    csend[...] = head_columns(cot, 0, False).astype(BF16)
    swap_c = remote(csend, cots.at[1], number("c"), sibling)
    swap_c.start()
    cots[0] = head_columns(cot, 0, True).astype(BF16)
    total = jnp.int32(0)
    for i in range(NDOC):
        starts[0, i] = jnp.full((8, HEAD), total.astype(F32))
        total = total + lens[0, i]
    swap_s = remote(starts.at[0], starts.at[1], number("s"), sibling)
    swap_s.start()

    swap_w.wait_recv()
    for p, (a1, a2, a3) in enumerate(ORDERS):
        mine = head_columns(w, p, True)
        other = wrecv[:, p * HEAD : (p + 1) * HEAD]
        both = jnp.where(first, jnp.concatenate([mine, other], 0), jnp.concatenate([other, mine], 0))
        wg[p][me[a3], me[a2], me[a1]] = both.astype(BF16)
        block = wg[p].at[me[a3], me[a2], me[a1]]
        index = number("g1", p)

        def one(k, _, block=block, a1=a1, index=index):
            remote(block, block, index, at(a1, along(a1, k))).start()
            return 0

        lax.fori_loop(1, size[a1], one, 0)

    def turn_own(i, _):
        at_chunk = pl.ds(pl.multiple_of(i * chunk, chunk), chunk)
        xt[at_chunk, 0:rows] = tok[:, at_chunk].T
        return 0

    def turn_sibling(i, _):
        at_chunk = pl.ds(pl.multiple_of(i * chunk, chunk), chunk)
        xt[at_chunk, rows : 2 * rows] = xsib[:, at_chunk].T
        return 0

    lax.fori_loop(0, seqs, turn_own, 0)
    for p, (a1, a2, a3) in enumerate(ORDERS):
        drain(wg[p].at[0, 0, pl.ds(0, size[a1] - 1)], recv_sem.at[number("g1", p)])
        block = wg[p].at[me[a3], me[a2]]
        index = number("g2", p)

        def two(k, _, block=block, a2=a2, index=index):
            remote(block, block, index, at(a2, along(a2, k))).start()
            return 0

        lax.fori_loop(1, size[a2], two, 0)
    swap_x.wait_recv()
    lax.fori_loop(0, seqs, turn_sibling, 0)

    def piece(p, sub):
        span = size[ORDERS[p][1]] // subs[p]
        return pl.ds(sub * span, span)

    def half(p, sign):
        return range(subs[p] // 2) if sign > 0 else range(subs[p] // 2, subs[p])

    lists = []
    for p in range(3):
        steps = size[ORDERS[p][2]] // 2
        for sign in (1, -1):
            hops = [(k, sub) for k in range(steps - 1) for sub in range(subs[p])]
            hops += [(steps - 1, sub) for sub in half(p, sign)]
            lists.append((p, sign, hops))
    going = {}
    waited = set()
    started = set()
    for turn in range(max(len(hops) for _, _, hops in lists)):
        for p, sign, hops in lists:
            if turn >= len(hops):
                continue
            k, sub = hops[turn]
            a1, a2, a3 = ORDERS[p]
            if p not in started:
                started.add(p)
                drain(wg[p].at[0, pl.ds(0, size[a2] - 1)], recv_sem.at[number("g2", p)])
            if k > 0:
                going[p, sign, k - 1, sub].wait_recv()
                waited.add((p, sign, k - 1, sub))
            block = wg[p].at[along(a3, -sign * k), piece(p, sub)]
            copy = remote(block, block, number("g3", p, sign, k, sub), at(a3, along(a3, sign)))
            copy.start()
            going[p, sign, k, sub] = copy

    swap_s.wait_recv()
    base = (s * rows).astype(F32)

    def count(b, positions):
        found = jnp.full(positions.shape, -1.0, F32)
        for i in range(NDOC):
            found = found + jnp.where(starts[b, i][None] <= positions, 1.0, 0.0)
        return found

    here = jnp.where(s < seqs // 2, starts[0], starts[1])

    def fill(r, _):
        low = (r * rows).astype(F32)
        inside = jnp.where((here >= low) & (here < low + rows), 1.0, 0.0)
        none = 1.0 - jnp.max(inside, axis=0)
        keep[r] = jnp.concatenate([none] * (keep.shape[1] // 8), axis=0)
        return 0

    lax.fori_loop(0, seqs, fill, 0)
    square = (rows // 8, 8, rows)
    by_row = lax.broadcasted_iota(jnp.int32, square, 0) * 8 + lax.broadcasted_iota(jnp.int32, square, 1)
    by_lane = lax.broadcasted_iota(jnp.int32, square, 2)

    def masks(b):
        docs_row = count(b, base + by_row.astype(F32))
        docs_lane = count(b, base + by_lane.astype(F32))
        linked = (docs_row == docs_lane) & (by_lane <= by_row)
        before = count(b, jnp.full((1, 8, HEAD), base - 1.0, F32))
        last = count(b, jnp.full((1, 8, HEAD), base + (rows - 1.0), F32))
        for i, found in enumerate((linked, docs_row == before, docs_row == last)):
            mask[b, i] = jnp.where(found, 1.0, 0.0).reshape(rows, rows)

    masks(0)
    masks(1)
    swap_c.wait_recv()
    for key, copy in going.items():
        if key not in waited:
            copy.wait_recv()
    for copy in going.values():
        copy.wait_send()
    for p, (a1, a2, a3) in enumerate(ORDERS):
        drain(wg[p].at[0, 0, pl.ds(0, size[a1] - 1)], send_sem.at[number("g1", p)])
        drain(wg[p].at[0, pl.ds(0, size[a2] - 1)], send_sem.at[number("g2", p)])
    for copy in (swap_w, swap_x, swap_c, swap_s):
        copy.wait_send()

    proj32 = gown

    def project(zz, acc):
        for xh in range(2):
            x2 = pl.ds(2 * xh, 2)
            parts = [
                wg[0][zz, :, x2].reshape(chunk, HEAD),
                wg[1][:, x2, zz].reshape(chunk, HEAD),
                jnp.stack([wg[2][2 * xh, zz], wg[2][2 * xh + 1, zz]], axis=1).reshape(chunk, HEAD),
            ]
            piece_w = jnp.concatenate(parts, axis=1)
            wfull[zz * 2 + xh] = piece_w
            at_chunk = pl.ds(pl.multiple_of((zz * 2 + xh) * chunk, chunk), chunk)
            acc = (acc[0] + dot(tok[:, at_chunk], piece_w), acc[1] + dot(xsib[:, at_chunk], piece_w))
        return acc

    zero = jnp.zeros((rows, 3 * HEAD), F32)
    acc = lax.fori_loop(0, size["z"], project, (zero, zero))
    for b in range(2):
        proj[b] = acc[b].astype(BF16)

    shrink = 1.0 / HEAD
    def block(b, p):
        return proj[b, :, p * HEAD : (p + 1) * HEAD]

    slices = seqs
    deep = 2 * HEAD // slices

    def exchange(source, target, key):
        index = number(key)

        def send(k, _):
            place = lax.rem(s + k, seqs)
            remote(scan.at[source, place], scan.at[target, s], index, (place, d)).start()
            return 0

        lax.fori_loop(1, seqs, send, 0)
        scan[target, s] = scan[source, s]
        drain(scan.at[target, pl.ds(0, seqs - 1)], recv_sem.at[index])
        drain(scan.at[source, pl.ds(0, seqs - 1)], send_sem.at[index])

    def carry(first_slot, key, backward):
        exchange(first_slot, first_slot + 1, key + "1")

        def step(i, run):
            r = seqs - 1 - i if backward else i
            scan[first_slot + 2, r] = run.astype(BF16)
            return run * keep[r] + scan[first_slot + 1, r].astype(F32)

        lax.fori_loop(0, seqs, step, jnp.zeros((deep, HEAD), F32))
        exchange(first_slot + 2, first_slot + 3, key + "2")
        return scan[first_slot + 3].reshape(2, HEAD, HEAD)

    def give(slot, b, state):
        scan[slot, pl.ds(b * slices // 2, slices // 2)] = state.astype(BF16).reshape(slices // 2, deep, HEAD)

    for b in range(2):
        weak[b] = (mask[b, 0] * (shrink * dot_nt(block(b, 0), block(b, 1)))).astype(BF16)
        tail = (mask[b, 2] * block(b, 1).astype(F32)).astype(BF16)
        give(0, b, dot_tn(tail, block(b, 2)))
        hold[b] = dot(weak[b], block(b, 2))
    incoming = carry(0, "f", False)

    for b in range(2):
        leading = mask[b, 1]
        q, k, v = block(b, 0), block(b, 1), block(b, 2)
        attended = hold[b] + leading * (shrink * dot(q, incoming[b]))
        inverse = lax.rsqrt(jnp.mean(attended * attended, axis=1, keepdims=True) + 1.0)
        result = (attended * inverse).astype(BF16)
        if b == 0:
            kept_n[...] = result
        else:
            nsend[...] = result
        upstream = cots[b].astype(F32)
        mean = jnp.mean(upstream * attended, axis=1, keepdims=True)
        grad = (inverse * upstream - attended * (inverse * inverse * inverse * mean)).astype(BF16)
        head = (leading * q.astype(F32)).astype(BF16)
        give(4, b, dot_tn(head, grad))
        mixed = (mask[b, 0] * (shrink * dot_nt(grad, v))).astype(BF16)
        grad_q = dot(mixed, k) + leading * (shrink * dot_nt(grad, incoming[b]))
        gbuf[b, :, 0:HEAD] = grad_q.astype(BF16)
        held[b, 0] = dot_tn(mixed, q)
        held[b, 1] = dot_tn(weak[b], grad)
    swap_n = remote(nsend, nrecv, number("n"), sibling)
    swap_n.start()
    arriving = carry(4, "r", True)
    for b in range(2):
        trailing = mask[b, 2] * shrink
        grad_k = held[b, 0] + trailing * dot_nt(block(b, 2), arriving[b])
        grad_v = held[b, 1] + trailing * dot(block(b, 1), arriving[b])
        gbuf[b, :, HEAD : 2 * HEAD] = grad_k.astype(BF16)
        gbuf[b, :, 2 * HEAD :] = grad_v.astype(BF16)

    def outer(zz, _):
        for xh in range(2):
            x2 = pl.ds(2 * xh, 2)
            at_chunk = pl.ds(pl.multiple_of((zz * 2 + xh) * chunk, chunk), chunk)
            part = dot(xt[at_chunk, :], gbuf[...].reshape(2 * rows, 3 * HEAD)).astype(BF16)
            parts = [part[:, p * HEAD : (p + 1) * HEAD].reshape(size["y"], 2, ROWS, HEAD) for p in range(3)]
            pg[0][zz, :, x2] = parts[0]
            pg[1][:, x2, zz] = parts[1]
            for xl in range(2):
                pg[2][2 * xh + xl, zz] = parts[2][:, xl]
        return 0

    lax.fori_loop(0, size["z"], outer, 0)

    def inner(i, _):
        at_chunk = pl.ds(pl.multiple_of(i * chunk, chunk), chunk)
        part = dot_nt(gbuf[...].reshape(2 * rows, 3 * HEAD), wfull[i])
        gown[:, at_chunk] = part[:rows]
        gsend[:, at_chunk] = part[rows:].astype(BF16)
        return 0

    lists = []
    for p in range(3):
        steps = size[ORDERS[p][2]] // 2
        for sign in (1, -1):
            far_half = list(half(p, sign))
            hops = [(0, sub) for sub in far_half]
            if steps > 1:
                hops += [(1, sub) for sub in range(subs[p]) if sub not in far_half]
                hops += [(1, sub) for sub in far_half]
            hops += [(k, sub) for k in range(2, steps) for sub in range(subs[p])]
            lists.append((p, sign, hops))
    coming = {}

    def slot(p, sign, k, sub):
        return ring[p].at[0 if sign > 0 else 1, k, piece(p, sub)]

    def add(target, source):
        target[...] = (target[...].astype(F32) + source[...].astype(F32)).astype(BF16)

    turns = max(len(hops) for _, _, hops in lists)
    done = 0
    for turn in range(turns):
        for p, sign, hops in lists:
            if turn >= len(hops):
                continue
            k, sub = hops[turn]
            a3 = ORDERS[p][2]
            steps = size[a3] // 2
            mine = pg[p].at[along(a3, sign * (steps - k)), piece(p, sub)]
            if (p, sign, k - 1, sub) in coming:
                coming[p, sign, k - 1, sub].wait_recv()
                add(mine, slot(p, sign, k - 1, sub))
            copy = remote(mine, slot(p, sign, k, sub), number("r3", p, sign, k, sub), at(a3, along(a3, sign)))
            copy.start()
            coming[p, sign, k, sub] = copy
        upto = min(seqs, -(-seqs * (turn + 1) // (turns - 1)))
        if upto > done:
            lax.fori_loop(done, upto, inner, 0)
            done = upto
    swap_g = remote(gsend, grecv, number("gi"), sibling)
    swap_g.start()
    for p, (a1, a2, a3) in enumerate(ORDERS):
        steps = size[a3] // 2
        for sub in range(subs[p]):
            mine = pg[p].at[me[a3], piece(p, sub)]
            for sign in (1, -1):
                if (p, sign, steps - 1, sub) in coming:
                    coming[p, sign, steps - 1, sub].wait_recv()
            both = [slot(p, sign, steps - 1, sub)[...].astype(F32) for sign in (1, -1) if (p, sign, steps - 1, sub) in coming]
            mine[...] = functools.reduce(lambda a, b: a + b, both, mine[...].astype(F32)).astype(BF16)
        index = number("r2", p)

        def three(k, _, p=p, a2=a2, a3=a3, index=index):
            place = along(a2, k)
            remote(pg[p].at[me[a3], place], far[p].at[me[a2]], index, at(a2, place)).start()
            return 0

        lax.fori_loop(1, size[a2], three, 0)

    swap_n.wait_recv()
    mine, other = kept_n[...].astype(F32), nrecv[...].astype(F32)
    normed[:, :HEAD] = jnp.where(first, mine, other).astype(BF16)
    normed[:, HEAD:] = jnp.where(first, other, mine).astype(BF16)
    for p, (a1, a2, a3) in enumerate(ORDERS):
        drain(far[p].at[pl.ds(0, size[a2] - 1)], recv_sem.at[number("r2", p)])
        mine = pg[p].at[me[a3], me[a2]]
        total = mine[...].astype(F32)
        for k in range(1, size[a2]):
            total = total + far[p][along(a2, k)].astype(F32)
        mine[...] = total.astype(BF16)
        index = number("r1", p)

        def four(k, _, p=p, a1=a1, mine=mine, index=index):
            place = along(a1, k)
            remote(mine.at[place], near[p].at[me[a1]], index, at(a1, place)).start()
            return 0

        lax.fori_loop(1, size[a1], four, 0)

    swap_g.wait_recv()

    def close(i, _):
        at_chunk = pl.ds(pl.multiple_of(i * chunk, chunk), chunk)
        gin[:, at_chunk] = (gown[:, at_chunk] + grecv[:, at_chunk].astype(F32)).astype(BF16)
        return 0

    lax.fori_loop(0, seqs, close, 0)
    factor = 1.0 / math.sqrt(size["y"] * 4 * seqs * rows)
    kept = []
    for p, (a1, a2, a3) in enumerate(ORDERS):
        drain(near[p].at[pl.ds(0, size[a1] - 1)], recv_sem.at[number("r1", p)])
        total = pg[p][me[a3], me[a2], me[a1]].astype(F32)
        for k in range(1, size[a1]):
            total = total + near[p][along(a1, k)].astype(F32)
        total = factor * total
        kept.append(jnp.where(first, total[:8], total[8:]))
        dsend[:, p * HEAD : (p + 1) * HEAD] = jnp.where(first, total[8:], total[:8])
    swap_d = remote(dsend, drecv, number("d"), sibling)
    swap_d.start()
    for copy in coming.values():
        copy.wait_send()
    for p, (a1, a2, a3) in enumerate(ORDERS):
        drain(far[p].at[pl.ds(0, size[a2] - 1)], send_sem.at[number("r2", p)])
        drain(near[p].at[pl.ds(0, size[a1] - 1)], send_sem.at[number("r1", p)])
    swap_n.wait_send()
    swap_g.wait_send()
    swap_d.wait()
    columns = []
    for p in range(3):
        other = drecv[:, p * HEAD : (p + 1) * HEAD]
        columns += [jnp.where(first, kept[p], other), jnp.where(first, other, kept[p])]
    gw[...] = jnp.concatenate(columns, axis=1).astype(BF16)


def solution(mesh):
    seqs, dps = mesh.shape["seq"], mesh.shape["dp"]
    size = {"x": 4, "y": dps // 4, "z": seqs // 2}
    subs = (2, 2, 4)

    def shards(inputs, weights, lengths, cotangent):
        tokens = inputs[0]
        rows, width = tokens.shape
        chunk = width // seqs
        wide = 3 * HEAD
        shapes = []
        for order in ORDERS:
            shapes.append(tuple(size[a] for a in order[::-1]) + (ROWS, HEAD))
        scratch = [
            pltpu.VMEM((rows, width), BF16),
            pltpu.VMEM((width, 2 * rows), BF16),
            pltpu.VMEM((seqs, chunk, wide), BF16),
            pltpu.VMEM((8, wide), F32),
            pltpu.VMEM((8, wide), F32),
            pltpu.VMEM((2, NDOC, 8, HEAD), F32),
            pltpu.VMEM((rows, HEAD), BF16),
            pltpu.VMEM((2, rows, HEAD), BF16),
            pltpu.VMEM((2, rows, wide), BF16),
            pltpu.VMEM((8, seqs, 2 * HEAD // seqs, HEAD), BF16),
            pltpu.VMEM((seqs, 2 * HEAD // seqs, HEAD), F32),
            pltpu.VMEM((2, rows, wide), BF16),
            pltpu.VMEM((2, 3, rows, rows), F32),
            pltpu.VMEM((2, rows, rows), BF16),
            pltpu.VMEM((2, rows, HEAD), F32),
            pltpu.VMEM((2, 2, rows, HEAD), F32),
            pltpu.VMEM((rows, HEAD), BF16),
            pltpu.VMEM((rows, HEAD), BF16),
            pltpu.VMEM((rows, HEAD), BF16),
            pltpu.VMEM((rows, width), F32),
            pltpu.VMEM((rows, width), BF16),
            pltpu.VMEM((rows, width), BF16),
            pltpu.VMEM((8, wide), F32),
            pltpu.VMEM((8, wide), F32),
            pltpu.SemaphoreType.DMA((120,)),
            pltpu.SemaphoreType.DMA((120,)),
        ]
        scratch += [pltpu.VMEM(shape, BF16) for shape in shapes]
        scratch += [pltpu.VMEM(shape, BF16) for shape in shapes]
        scratch += [pltpu.VMEM((2, shape[0] // 2) + shape[1:], BF16) for shape in shapes]
        scratch += [pltpu.VMEM(shape[1:], BF16) for shape in shapes]
        scratch += [pltpu.VMEM(shape[2:], BF16) for shape in shapes]
        vmem = pl.BlockSpec(memory_space=pltpu.VMEM)
        normed, gin, gw = pl.pallas_call(
            functools.partial(kernel, size, subs),
            out_shape=(
                jax.ShapeDtypeStruct((rows, 2 * HEAD), BF16),
                jax.ShapeDtypeStruct((rows, width), BF16),
                jax.ShapeDtypeStruct((8, 2 * wide), BF16),
            ),
            in_specs=[vmem, vmem, pl.BlockSpec(memory_space=pltpu.SMEM), vmem],
            out_specs=(vmem, vmem, vmem),
            scratch_shapes=scratch,
            compiler_params=pltpu.CompilerParams(
                collective_id=0, has_side_effects=True, vmem_limit_bytes=48 * 1024 * 1024
            ),
            cost_estimate=pl.CostEstimate(flops=3 * 10**9, bytes_accessed=4 * 10**6, transcendentals=0),
        )(tokens, weights, lengths, cotangent[0])
        return normed[None], gin[None], gw

    placed = (P("dp", "seq", None), P(("seq", "dp"), None), P("dp", None), P("dp", "seq", None))
    return jax.shard_map(
        shards,
        mesh=mesh,
        in_specs=placed,
        out_specs=(P("dp", "seq", None), P("dp", "seq", None), P(("seq", "dp"), None)),
        check_vma=False,
    )
```

time: 1310 us -> 119 us (0.09)
  waiting for transfers between devices: 1170 us -> 0 us
  Pallas kernels: 0 us -> 113 us
  blocking collectives: 62.6 us -> 0 us
  other arithmetic: 37.1 us -> 0 us
  matrix products: 17 us -> 0 us
  between operations: 15.2 us -> 0.65 us
    all_gather x4 -> x0, waiting for transfers between devices: 1060 us -> none  [the longest x1 816 us: shards(): piece = lax.all_gather(weights, ('seq', 'dp'), axis=0, tiled=True)]
    pallas_call x0 -> x1, Pallas kernels: none -> 113 us  [shards(): pl.pallas_call(functools.partial(kernel, size, subs), out_shape=(jax.Shap...]
    unnamed x6 -> x0, waiting for transfers between devices: 109 us -> none
    unnamed x1 -> x0, blocking collectives: 32.9 us -> none
    all_to_all x1 -> x0, blocking collectives: 29.7 us -> none  [shards(): lax.all_to_all(tokens, 'seq', split_axis=1, concat_axis=0, tiled=True)]
    select_n x15 -> x0, other arithmetic: 23.9 us -> none  [chain_combine(): jnp.where(later[1] > 0, later[0], earlier[0] + later[0])]
    dot_general x15 -> x0, matrix products: 17 us -> none  [the longest x1 5.93 us: shards(): lax.dot_general(grad_all, piece, (((1,), (1,)), ((), ())), preferred_elem...]
  transfers between devices with their start and end apart: 5 -> 0, of which waited for: 5 -> 0; matrix products, arithmetic and copies ran while one was open for 1% -> 0% of each run, Pallas kernels for 0% -> 0%
where the time goes in v1:
time: 119 us
  Pallas kernels  113 us (95%)
  local copies, waits for them, and re-layouts  5.62 us (5%)
    pallas_call x1, Pallas kernels, shards(): pl.pallas_call(functools.partial(kernel, size, subs), out_shape=(jax.Shap...  113 us
    unnamed x11, local copies, waits for them, and re-layouts  5.62 us

profile of v1, /device:TPU:1, one launch (start us, length us, event | category | flops | bytes accessed | tf_op | source)
XLA Modules:
  0.0 118.9 jit_solution(8261315158784064066)
XLA Ops:
  0.6 0.0 copy-start.3
  0.6 0.6 copy-done.3
  1.3 0.0 copy-start
  1.3 1.2 %copy-done = bf16[1,128,4096]{2,1,0:T(8,128)(2,1)S(1)} copy-done((bf16[1,128,4096]{2,1,0:T(8,128)(2,1)S(1)}, bf16[1,128,4096]{2,1,0:T(8,128)(2,1)}, u32[]{:S(2)}) %copy-start) | copy-done | bytes 1048600
  2.5 0.0 copy-start.1
  2.5 0.8 copy-done.1
  3.4 0.0 copy-start.2
  3.4 0.7 copy-done.2
  4.1 112.6 %shard_map.67 = (bf16[128,256]{1,0:T(8,128)(2,1)S(1)}, bf16[128,4096]{1,0:T(8,128)(2,1)S(1)}, bf16[8,768]{1,0:T(8,128)(2,1)S(1)}) custom-call(bf16[128,4096]{1,0:T(8,128)(2,1)S(1)} %bitcast.6, bf16[8,768]{1,0:T(8,128)(2,1)S(1)} %copy-done.2, s32[1,8]{1,0:T(1,128)S(1)} %copy-done.3, bf16[128,256]{1,0:T(8,128)(2,1)S(1)} %bitcast.7), custom_call_target="tpu_custom_call" | custom-call | flops 3000000000 | bytes 4000000 | tf_op jit(solution)/shard_map/pallas_call | solution.py:501
  116.7 0.6 copy.10
  117.3 1.0 copy.11
  118.3 0.6 copy.12
Async XLA Ops:
  0.6 0.7 copy-start.3
  1.3 1.2 %copy-start = (bf16[1,128,4096]{2,1,0:T(8,128)(2,1)S(1)}, bf16[1,128,4096]{2,1,0:T(8,128)(2,1)}, u32[]{:S(2)}) copy-start(bf16[1,128,4096]{2,1,0:T(8,128)(2,1)} %param.4) | copy-start | bytes 3145732
  2.5 0.8 copy-start.1
  3.4 0.7 copy-start.2

commit v2 on v1

v2 whole, which is shorter than its diff:
```python
import functools
import math

import jax
import jax.numpy as jnp
from jax import lax
from jax.experimental import pallas as pl
from jax.experimental.pallas import tpu as pltpu
from jax.sharding import PartitionSpec as P

HEAD = 128
NDOC = 8
ROWS = 16
MESH = pl.DeviceIdType.MESH
F32, BF16 = jnp.float32, jnp.bfloat16
ORDERS = (("y", "z", "x"), ("x", "y", "z"), ("x", "z", "y"))


def dot(a, b):
    return jnp.dot(a, b, preferred_element_type=F32)


def dot_nt(a, b):
    return lax.dot_general(a, b, (((1,), (1,)), ((), ())), preferred_element_type=F32)


def dot_tn(a, b):
    return lax.dot_general(a, b, (((0,), (0,)), ((), ())), preferred_element_type=F32)


def kernel(size, tok_hbm, w_hbm, lens_hbm, cot_hbm, normed, gin, gw, *rest):
    (x2, w, cot, lens, xt, wq, wkv, wsend, wrecv, starts, csend, cots, proj, scan, keep, gbuf, mask, weak, hold, held,
     kept_n, nsend, nrecv, gown, gsend, grecv, dsend, drecv, load_sem, send_sem, recv_sem) = rest[:31]
    wg, pg, ring, far, near = (rest[31 + 3 * i : 34 + 3 * i] for i in range(5))
    seqs = 2 * size["z"]
    rows, width = x2.shape[1:]
    chunk = size["y"] * 2 * ROWS
    s, d = lax.axis_index("seq"), lax.axis_index("dp")
    c = lax.rem(d, 2)
    me = {"x": lax.rem(s, 2) * 2 + lax.rem(d // 2, 2), "y": d // 4, "z": s // 2}
    sibling = (s, d + 1 - 2 * c)
    first = c == 0

    def at(axis, place):
        spot = dict(me)
        spot[axis] = place
        return (spot["z"] * 2 + spot["x"] // 2, spot["y"] * 4 + lax.rem(spot["x"], 2) * 2 + c)

    def along(axis, step):
        return lax.rem(me[axis] + step + size[axis], size[axis])

    names, sends = {}, {}

    def remote(src, dst, arrival, departure, target):
        return pltpu.make_async_remote_copy(
            src_ref=src,
            dst_ref=dst,
            send_sem=send_sem.at[sends.setdefault(departure, len(sends))],
            recv_sem=recv_sem.at[names.setdefault(arrival, len(names))],
            device_id=target,
            device_id_type=MESH,
        )

    def arrived(ref, *key):
        pltpu.make_async_copy(ref, ref, recv_sem.at[names[key]]).wait()

    def departed(ref, *key):
        pltpu.make_async_copy(ref, ref, send_sem.at[sends[key]]).wait()

    loads = [
        pltpu.make_async_copy(w_hbm, w, load_sem.at[0]),
        pltpu.make_async_copy(tok_hbm, x2.at[0], load_sem.at[1]),
        pltpu.make_async_copy(lens_hbm, lens, load_sem.at[2]),
        pltpu.make_async_copy(cot_hbm, cot, load_sem.at[3]),
    ]
    for load in loads:
        load.start()

    barrier = pltpu.get_barrier_semaphore()

    def greet(target):
        pl.semaphore_signal(barrier, inc=1, device_id=target, device_id_type=MESH)

    greet(sibling)
    for k in range(1, seqs):
        greet((lax.rem(s + k, seqs), d))
    for k in range(1, size["y"]):
        greet(at("y", along("y", k)))
    greet(at("x", along("x", 1)))
    greet(at("x", along("x", -1)))

    def head_columns(ref, part, mine):
        left = ref[:, part * 2 * HEAD : (2 * part + 1) * HEAD].astype(F32)
        right = ref[:, (2 * part + 1) * HEAD : (2 * part + 2) * HEAD].astype(F32)
        return jnp.where(first == mine, left, right)

    loads[0].wait()
    for p in range(3):
        wsend[:, p * HEAD : (p + 1) * HEAD] = head_columns(w, p, False)

    def turn(b):
        def one(i, _):
            at_chunk = pl.ds(pl.multiple_of(i * chunk, chunk), chunk)
            xt[at_chunk, b * rows : (b + 1) * rows] = x2[b, :, at_chunk].T
            return 0

        return one

    base = (s * rows).astype(F32)
    square = (rows // 8, 8, rows)
    by_row = lax.broadcasted_iota(jnp.int32, square, 0) * 8 + lax.broadcasted_iota(jnp.int32, square, 1)
    by_lane = lax.broadcasted_iota(jnp.int32, square, 2)

    def count(b, positions):
        found = jnp.full(positions.shape, -1.0, F32)
        for i in range(NDOC):
            found = found + jnp.where(starts[b, i][None] <= positions, 1.0, 0.0)
        return found

    def masks(b):
        docs_row = count(b, base + by_row.astype(F32))
        docs_lane = count(b, base + by_lane.astype(F32))
        linked = (docs_row == docs_lane) & (by_lane <= by_row)
        before = count(b, jnp.full((1, 8, HEAD), base - 1.0, F32))
        last = count(b, jnp.full((1, 8, HEAD), base + (rows - 1.0), F32))
        for i, found in enumerate((linked, docs_row == before, docs_row == last)):
            mask[b, i] = jnp.where(found, 1.0, 0.0).reshape(rows, rows)

    pl.semaphore_wait(barrier, 1 + seqs - 1 + size["y"] - 1 + 2)

    swap_w = remote(wsend, wrecv, ("w",), ("w",), sibling)
    swap_s = remote(starts.at[0], starts.at[1], ("s",), ("s",), sibling)
    swap_c = remote(csend, cots.at[1], ("c",), ("c",), sibling)
    swap_x = remote(x2.at[0], x2.at[1], ("x",), ("x",), sibling)
    swap_w.start()

    def offsets(axis):
        n = size[axis]
        return sorted(range(n), key=lambda o: (min(o, n - o), o))

    swap_w.wait_recv()
    for p in (1, 2, 0):
        a1, a2, a3 = ORDERS[p]
        mine = head_columns(w, p, True)
        other = wrecv[:, p * HEAD : (p + 1) * HEAD]
        both = jnp.where(first, jnp.concatenate([mine, other], 0), jnp.concatenate([other, mine], 0))
        wg[p][me[a3], me[a2], me[a1]] = both.astype(BF16)
        block = wg[p].at[me[a3], me[a2], me[a1]]
        for o in offsets(a1)[1:]:
            remote(block, block, ("g1", p), ("g1", p), at(a1, along(a1, o))).start()

    for load in loads[1:]:
        load.wait()
    swap_x.start()
    csend[...] = head_columns(cot, 0, False).astype(BF16)
    swap_c.start()
    cots[0] = head_columns(cot, 0, True).astype(BF16)
    total = jnp.int32(0)
    for i in range(NDOC):
        starts[0, i] = jnp.full((8, HEAD), total.astype(F32))
        total = total + lens[0, i]
    swap_s.start()

    def second(p):
        a1, a2, a3 = ORDERS[p]
        arrived(wg[p].at[0, 0, pl.ds(0, size[a1] - 1)], "g1", p)
        block = wg[p].at[me[a3], me[a2]]
        for o in offsets(a2)[1:]:
            remote(block, block, ("g2", p, size[a2] - o), ("g2", p), at(a2, along(a2, o))).start()

    def halves(axis, sign, order):
        n = size[axis]
        return order[: n // 2] if sign > 0 else order[n // 2 :]

    going, waited, here, turned = {}, set(), set(), {}
    most = size["z"] // 2

    def part_of(sign):
        return pl.ds(0 if sign > 0 else size["y"] // 2, size["y"] // 2)

    def come_round(sign, k):
        if ("z", sign, k) not in here:
            here.add(("z", sign, k))
            turned[sign, k].wait_recv()

    def go_round(k):
        for sign in (1, -1):
            if k:
                come_round(sign, k - 1)
            block = wg[0].at[me["x"], along("z", -sign * k)]
            if k == most - 1:
                block = block.at[part_of(sign)]
            copy = remote(block, block, ("g2", 0, sign, k), ("g2", 0), at("z", along("z", sign)))
            copy.start()
            turned[sign, k] = copy

    def forward(p, sign, k, o):
        a1, a2, a3 = ORDERS[p]
        if p == 0 and k == 0 and o:
            hops = min(o, size[a2] - o)
            for way in (1, -1):
                if hops == most or (o > most) == (way > 0):
                    come_round(way, hops - 1)
        elif k == 0 and o and (p, o) not in here:
            here.add((p, o))
            arrived(wg[p].at[0, 0], "g2", p, o)
        if k > 0:
            going[p, sign, k - 1, o].wait_recv()
            waited.add((p, sign, k - 1, o))
        block = wg[p].at[along(a3, -sign * k), along(a2, o)]
        copy = remote(block, block, ("g3", p, sign, k, o), ("g3", p), at(a3, along(a3, sign)))
        copy.start()
        going[p, sign, k, o] = copy

    def gather_hops(p, sign):
        a1, a2, a3 = ORDERS[p]
        steps, order = size[a3] // 2, offsets(a2)
        return [(k, o) for k in range(steps - 1) for o in order] + [
            (steps - 1, o) for o in halves(a2, sign, order)
        ]

    def gathered(p):
        for key, copy in going.items():
            if key[0] == p and key not in waited:
                copy.wait_recv()

    second(1)
    second(2)
    masks(0)
    lax.fori_loop(0, seqs, turn(0), 0)
    lists = [(p, sign, gather_hops(p, sign)) for p in (1, 2) for sign in (1, -1)]
    for turn_at in range(max(len(hops) for _, _, hops in lists)):
        for p, sign, hops in lists:
            if turn_at < len(hops):
                forward(p, sign, *hops[turn_at])
        if turn_at == 3:
            arrived(wg[0].at[0, 0, pl.ds(0, size["y"] - 1)], "g1", 0)
        if turn_at % 8 == 3:
            go_round(turn_at // 8)
        if turn_at == size["y"] - 1:
            swap_x.wait_recv()
        if turn_at >= size["y"]:
            done = (turn_at - size["y"]) * 2
            if done < seqs:
                lax.fori_loop(done, done + 2, turn(1), 0)

    swap_s.wait_recv()
    masks(1)
    ours = jnp.where(s < seqs // 2, starts[0], starts[1])

    def fill(r, _):
        low = (r * rows).astype(F32)
        inside = jnp.where((ours >= low) & (ours < low + rows), 1.0, 0.0)
        none = 1.0 - jnp.max(inside, axis=0)
        keep[r] = jnp.concatenate([none] * (keep.shape[1] // 8), axis=0)
        return 0

    lax.fori_loop(0, seqs, fill, 0)
    swap_c.wait_recv()
    query_hops = {sign: gather_hops(0, sign) for sign in (1, -1)}
    early = [hop for hop in query_hops[1] if hop[0] == 0]
    for k, o in early:
        for sign in (1, -1):
            forward(0, sign, k, o)
    gathered(1)
    gathered(2)

    def tokens_of(zz):
        at_chunk = pl.ds(pl.multiple_of(zz * 2 * chunk, 2 * chunk), 2 * chunk)
        return x2[:, :, at_chunk].reshape(2 * rows, 2 * chunk)

    def project_kv(zz, acc):
        for xh in range(2):
            pair = pl.ds(2 * xh, 2)
            wkv[zz, xh * chunk : (xh + 1) * chunk, :HEAD] = wg[1][zz, :, pair].reshape(chunk, HEAD)
            wkv[zz, xh * chunk : (xh + 1) * chunk, HEAD:] = wg[2][:, zz, pair].reshape(chunk, HEAD)
        return acc + dot(tokens_of(zz), wkv[zz])

    def project_q(zz, acc):
        for xh in range(2):
            part = jnp.stack([wg[0][2 * xh, zz], wg[0][2 * xh + 1, zz]], axis=1).reshape(chunk, HEAD)
            wq[zz, xh * chunk : (xh + 1) * chunk] = part
        return acc + dot(tokens_of(zz), wq[zz])

    acc = lax.fori_loop(0, size["z"], project_kv, jnp.zeros((2 * rows, 2 * HEAD), F32))
    proj[:, :, HEAD:] = acc.astype(BF16).reshape(2, rows, 2 * HEAD)

    shrink = 1.0 / HEAD

    def block(b, p):
        return proj[b, :, p * HEAD : (p + 1) * HEAD]

    deep = 2 * HEAD // seqs

    def send_slices(source, key):
        def send(i, _):
            k = seqs // 2 + (2 * lax.rem(i, 2) - 1) * ((i + 1) // 2)
            place = lax.rem(s + k, seqs)
            remote(scan.at[source, place], scan.at[source + 1, s], (key,), (key,), (place, d)).start()
            return 0

        lax.fori_loop(0, seqs - 1, send, 0)
        scan[source + 1, s] = scan[source, s]

    def take_slices(source, key):
        arrived(scan.at[source + 1, pl.ds(0, seqs - 1)], key)

    def sweep(source, backward):
        def step(i, run):
            r = seqs - 1 - i if backward else i
            scan[source + 2, r] = run.astype(BF16)
            return run * keep[r] + scan[source + 1, r].astype(F32)

        lax.fori_loop(0, seqs, step, jnp.zeros((deep, HEAD), F32))

    def give(slot, b, state):
        scan[slot, pl.ds(b * seqs // 2, seqs // 2)] = state.astype(BF16).reshape(seqs // 2, deep, HEAD)

    for b in range(2):
        tail = (mask[b, 2] * block(b, 1).astype(F32)).astype(BF16)
        give(0, b, dot_tn(tail, block(b, 2)))
    send_slices(0, "f1")
    for sign in (1, -1):
        for k, o in query_hops[sign][len(early) :]:
            forward(0, sign, k, o)
    take_slices(0, "f1")
    sweep(0, False)
    send_slices(2, "f2")
    gathered(0)
    acc = lax.fori_loop(0, size["z"], project_q, jnp.zeros((2 * rows, HEAD), F32))
    proj[:, :, :HEAD] = acc.astype(BF16).reshape(2, rows, HEAD)
    for b in range(2):
        weak[b] = (mask[b, 0] * (shrink * dot_nt(block(b, 0), block(b, 1)))).astype(BF16)
        hold[b] = dot(weak[b], block(b, 2))
    take_slices(2, "f2")
    def state(slot, b):
        return scan[slot, pl.ds(b * seqs // 2, seqs // 2)].reshape(HEAD, HEAD)

    for b in range(2):
        leading = mask[b, 1]
        q = block(b, 0)
        attended = hold[b] + leading * (shrink * dot(q, state(3, b)))
        inverse = lax.rsqrt(jnp.mean(attended * attended, axis=1, keepdims=True) + 1.0)
        result = (attended * inverse).astype(BF16)
        if b == 0:
            kept_n[...] = result
        else:
            nsend[...] = result
        upstream = cots[b].astype(F32)
        mean = jnp.mean(upstream * attended, axis=1, keepdims=True)
        grad = (inverse * upstream - attended * (inverse * inverse * inverse * mean)).astype(BF16)
        cots[b] = grad
        head = (leading * q.astype(F32)).astype(BF16)
        give(4, b, dot_tn(head, grad))
    send_slices(4, "r1")
    swap_n = remote(nsend, nrecv, ("n",), ("n",), sibling)
    swap_n.start()
    for b in range(2):
        grad = cots[b]
        mixed = (mask[b, 0] * (shrink * dot_nt(grad, block(b, 2)))).astype(BF16)
        grad_q = dot(mixed, block(b, 1)) + mask[b, 1] * (shrink * dot_nt(grad, state(3, b)))
        gbuf[b, :, 0:HEAD] = grad_q.astype(BF16)
        held[b, 0] = dot_tn(mixed, block(b, 0))
        held[b, 1] = dot_tn(weak[b], grad)

    def outer_q(zz, _):
        at_chunk = pl.ds(pl.multiple_of(zz * 2 * chunk, 2 * chunk), 2 * chunk)
        part = dot(xt[at_chunk, :], gbuf[:, :, :HEAD].reshape(2 * rows, HEAD)).astype(BF16)
        part = part.reshape(2, size["y"], 2, ROWS, HEAD)
        for xh in range(2):
            for xl in range(2):
                pg[0][2 * xh + xl, zz] = part[xh, :, xl]
        return 0

    def outer_kv(zz, _):
        at_chunk = pl.ds(pl.multiple_of(zz * 2 * chunk, 2 * chunk), 2 * chunk)
        part = dot(xt[at_chunk, :], gbuf[:, :, HEAD:].reshape(2 * rows, 2 * HEAD)).astype(BF16)
        for xh in range(2):
            pair = pl.ds(2 * xh, 2)
            some = part[xh * chunk : (xh + 1) * chunk]
            pg[1][zz, :, pair] = some[:, :HEAD].reshape(size["y"], 2, ROWS, HEAD)
            pg[2][:, zz, pair] = some[:, HEAD:].reshape(size["y"], 2, ROWS, HEAD)
        return 0

    def inner(i, _):
        at_chunk = pl.ds(pl.multiple_of(i * 2 * chunk, 2 * chunk), 2 * chunk)
        part = dot_nt(gbuf[:, :, :HEAD].reshape(2 * rows, HEAD), wq[i])
        part = part + dot_nt(gbuf[:, :, HEAD:].reshape(2 * rows, 2 * HEAD), wkv[i])
        gown[:, at_chunk] = part[:rows]
        gsend[:, at_chunk] = part[rows:].astype(BF16)
        return 0

    def sum_hops(p, sign):
        a1, a2, a3 = ORDERS[p]
        steps, order = size[a3] // 2, offsets(a2)[::-1]
        some = halves(a2, sign, order)
        hops = [(0, o) for o in some]
        if steps > 1:
            hops += [(1, o) for o in order if o not in some] + [(1, o) for o in some]
        return hops + [(k, o) for k in range(2, steps) for o in order]

    coming = {}

    def slot(p, sign, k, o):
        return ring[p].at[0 if sign > 0 else 1, k, along(ORDERS[p][1], o)]

    def pass_on(p, sign, k, o):
        a1, a2, a3 = ORDERS[p]
        mine = pg[p].at[along(a3, sign * (size[a3] // 2 - k)), along(a2, o)]
        if (p, sign, k - 1, o) in coming:
            coming[p, sign, k - 1, o].wait_recv()
            mine[...] = (mine[...].astype(F32) + slot(p, sign, k - 1, o)[...].astype(F32)).astype(BF16)
        copy = remote(mine, slot(p, sign, k, o), ("r3", p, sign, k, o), ("r3", p), at(a3, along(a3, sign)))
        copy.start()
        coming[p, sign, k, o] = copy

    def settle(p, o):
        a1, a2, a3 = ORDERS[p]
        mine = pg[p].at[me[a3], along(a2, o)]
        total = mine[...].astype(F32)
        for sign in (1, -1):
            key = (p, sign, size[a3] // 2 - 1, o)
            if key in coming:
                coming[key].wait_recv()
                total = total + slot(*key)[...].astype(F32)
        mine[...] = total.astype(BF16)
        if o and p:
            remote(mine, far[p].at[me[a2]], ("r2", p), ("r2", p), at(a2, along(a2, o))).start()

    summing = {}

    def sum_round(k):
        for sign in (1, -1):
            mine = pg[0].at[me["x"], along("z", sign * (most - k))]
            base_slot = 0 if sign > 0 else most
            there = far[0].at[base_slot + k]
            if k:
                summing[sign, k - 1].wait_recv()
                rows_in = part_of(sign) if k == 1 else pl.ds(0, size["y"])
                piece = mine.at[rows_in]
                came = far[0][base_slot + k - 1, rows_in].astype(F32)
                piece[...] = (piece[...].astype(F32) + came).astype(BF16)
            else:
                mine, there = mine.at[part_of(sign)], there.at[part_of(sign)]
            copy = remote(mine, there, ("r2", 0, sign, k), ("r2", 0), at("z", along("z", sign)))
            copy.start()
            summing[sign, k] = copy

    def first_sends(p, total):
        a1, a2, a3 = ORDERS[p]
        mine = pg[p].at[me[a3], me[a2]]
        mine[...] = total.astype(BF16)
        for o in offsets(a1)[:0:-1]:
            place = along(a1, o)
            remote(mine.at[place], near[p].at[me[a1]], ("r1", p), ("r1", p), at(a1, place)).start()

    def sum_end():
        total = pg[0][me["x"], me["z"]].astype(F32)
        for sign in (1, -1):
            summing[sign, most - 1].wait_recv()
            total = total + far[0][(0 if sign > 0 else most) + most - 1].astype(F32)
        first_sends(0, total)

    def settle_second(p):
        a1, a2, a3 = ORDERS[p]
        arrived(far[p].at[pl.ds(0, size[a2] - 1)], "r2", p)
        mine = pg[p].at[me[a3], me[a2]]
        total = mine[...].astype(F32)
        for k in range(1, size[a2]):
            total = total + far[p][along(a2, k)].astype(F32)
        first_sends(p, total)

    lax.fori_loop(0, size["z"], outer_q, 0)
    steps_q = {sign: sum_hops(0, sign) for sign in (1, -1)}
    free = size[ORDERS[0][1]]
    for i in range(free):
        for sign in (1, -1):
            pass_on(0, sign, *steps_q[sign][i])
    take_slices(4, "r1")
    sweep(4, True)
    send_slices(6, "r2s")
    for i in range(free, len(steps_q[1])):
        for sign in (1, -1):
            pass_on(0, sign, *steps_q[sign][i])
    take_slices(6, "r2s")
    for b in range(2):
        trailing = mask[b, 2] * shrink
        grad_k = held[b, 0] + trailing * dot_nt(block(b, 2), state(7, b))
        grad_v = held[b, 1] + trailing * dot(block(b, 1), state(7, b))
        gbuf[b, :, HEAD : 2 * HEAD] = grad_k.astype(BF16)
        gbuf[b, :, 2 * HEAD :] = grad_v.astype(BF16)
    lax.fori_loop(0, size["z"], outer_kv, 0)

    lists = [(p, sign, sum_hops(p, sign)) for p in (1, 2) for sign in (1, -1)]
    turns = max(len(hops) for _, _, hops in lists)
    done = 0
    for turn_at in range(turns):
        for p, sign, hops in lists:
            if turn_at < len(hops):
                pass_on(p, sign, *hops[turn_at])
        upto = min(size["z"], -(-size["z"] * (turn_at + 1) * 4 // (turns * 3)))
        if upto > done:
            lax.fori_loop(done, upto, inner, 0)
            done = upto
        if turn_at == 1:
            for o in offsets(ORDERS[0][1])[::-1]:
                settle(0, o)
        if turn_at % 8 == 1:
            sum_round(turn_at // 8)
    swap_g = remote(gsend, grecv, ("gi",), ("gi",), sibling)
    swap_g.start()
    for o in offsets(ORDERS[1][1])[::-1]:
        settle(1, o)
        settle(2, o)
    sum_end()
    swap_n.wait_recv()
    mine, other = kept_n[...].astype(F32), nrecv[...].astype(F32)
    normed[:, :HEAD] = jnp.where(first, mine, other).astype(BF16)
    normed[:, HEAD:] = jnp.where(first, other, mine).astype(BF16)
    settle_second(1)
    settle_second(2)
    swap_g.wait_recv()

    def close(i, _):
        at_chunk = pl.ds(pl.multiple_of(i * chunk, chunk), chunk)
        gin[:, at_chunk] = (gown[:, at_chunk] + grecv[:, at_chunk].astype(F32)).astype(BF16)
        return 0

    lax.fori_loop(0, seqs, close, 0)
    factor = 1.0 / math.sqrt(size["y"] * 4 * seqs * rows)
    kept = []
    for p, (a1, a2, a3) in enumerate(ORDERS):
        arrived(near[p].at[pl.ds(0, size[a1] - 1)], "r1", p)
        total = pg[p][me[a3], me[a2], me[a1]].astype(F32)
        for k in range(1, size[a1]):
            total = total + near[p][along(a1, k)].astype(F32)
        total = factor * total
        kept.append(jnp.where(first, total[:8], total[8:]))
        dsend[:, p * HEAD : (p + 1) * HEAD] = jnp.where(first, total[8:], total[:8])
    swap_d = remote(dsend, drecv, ("d",), ("d",), sibling)
    swap_d.start()
    for p, (a1, a2, a3) in enumerate(ORDERS):
        departed(wg[p].at[0, 0, pl.ds(0, size[a1] - 1)], "g1", p)
        departed(wg[p].at[0, pl.ds(0, size[a2] - 1)], "g2", p)
        departed(wg[p].at[pl.ds(0, size[a3] - 1)], "g3", p)
        departed(pg[p].at[pl.ds(0, size[a3] - 1)], "r3", p)
        departed(far[p].at[pl.ds(0, size[a2] - 1)], "r2", p)
        departed(near[p].at[pl.ds(0, size[a1] - 1)], "r1", p)
    for i, key in enumerate(("f1", "f2", "r1", "r2s")):
        departed(scan.at[2 * i, pl.ds(0, seqs - 1)], key)
    for copy in (swap_w, swap_x, swap_c, swap_s, swap_n, swap_g):
        copy.wait_send()
    swap_d.wait()
    columns = []
    for p in range(3):
        other = drecv[:, p * HEAD : (p + 1) * HEAD]
        columns += [jnp.where(first, kept[p], other), jnp.where(first, other, kept[p])]
    gw[...] = jnp.concatenate(columns, axis=1).astype(BF16)
    assert len(names) <= recv_sem.shape[0] and len(sends) <= send_sem.shape[0]


def solution(mesh):
    seqs, dps = mesh.shape["seq"], mesh.shape["dp"]
    size = {"x": 4, "y": dps // 4, "z": seqs // 2}

    def shards(inputs, weights, lengths, cotangent):
        tokens = inputs[0]
        rows, width = tokens.shape
        chunk = width // seqs
        wide = 3 * HEAD
        shapes = []
        for order in ORDERS:
            shapes.append(tuple(size[a] for a in order[::-1]) + (ROWS, HEAD))
        scratch = [
            pltpu.VMEM((2, rows, width), BF16),
            pltpu.VMEM((8, 2 * wide), BF16),
            pltpu.VMEM((rows, 2 * HEAD), BF16),
            pltpu.SMEM((1, NDOC), jnp.int32),
            pltpu.VMEM((width, 2 * rows), BF16),
            pltpu.VMEM((seqs // 2, 2 * chunk, HEAD), BF16),
            pltpu.VMEM((seqs // 2, 2 * chunk, 2 * HEAD), BF16),
            pltpu.VMEM((8, wide), F32),
            pltpu.VMEM((8, wide), F32),
            pltpu.VMEM((2, NDOC, 8, HEAD), F32),
            pltpu.VMEM((rows, HEAD), BF16),
            pltpu.VMEM((2, rows, HEAD), BF16),
            pltpu.VMEM((2, rows, wide), BF16),
            pltpu.VMEM((8, seqs, 2 * HEAD // seqs, HEAD), BF16),
            pltpu.VMEM((seqs, 2 * HEAD // seqs, HEAD), F32),
            pltpu.VMEM((2, rows, wide), BF16),
            pltpu.VMEM((2, 3, rows, rows), F32),
            pltpu.VMEM((2, rows, rows), BF16),
            pltpu.VMEM((2, rows, HEAD), F32),
            pltpu.VMEM((2, 2, rows, HEAD), F32),
            pltpu.VMEM((rows, HEAD), BF16),
            pltpu.VMEM((rows, HEAD), BF16),
            pltpu.VMEM((rows, HEAD), BF16),
            pltpu.VMEM((rows, width), F32),
            pltpu.VMEM((rows, width), BF16),
            pltpu.VMEM((rows, width), BF16),
            pltpu.VMEM((8, wide), F32),
            pltpu.VMEM((8, wide), F32),
            pltpu.SemaphoreType.DMA((4,)),
            pltpu.SemaphoreType.DMA((40,)),
            pltpu.SemaphoreType.DMA((352,)),
        ]
        scratch += [pltpu.VMEM(shape, BF16) for shape in shapes]
        scratch += [pltpu.VMEM(shape, BF16) for shape in shapes]
        scratch += [pltpu.VMEM((2, shape[0] // 2) + shape[1:], BF16) for shape in shapes]
        scratch += [pltpu.VMEM(shape[1:], BF16) for shape in shapes]
        scratch += [pltpu.VMEM(shape[2:], BF16) for shape in shapes]
        vmem = pl.BlockSpec(memory_space=pltpu.VMEM)
        normed, gin, gw = pl.pallas_call(
            functools.partial(kernel, size),
            out_shape=(
                jax.ShapeDtypeStruct((rows, 2 * HEAD), BF16),
                jax.ShapeDtypeStruct((rows, width), BF16),
                jax.ShapeDtypeStruct((8, 2 * wide), BF16),
            ),
            in_specs=[pl.BlockSpec(memory_space=pltpu.HBM)] * 4,
            out_specs=(vmem, vmem, vmem),
            scratch_shapes=scratch,
            compiler_params=pltpu.CompilerParams(
                collective_id=0, has_side_effects=True, vmem_limit_bytes=48 * 1024 * 1024
            ),
            cost_estimate=pl.CostEstimate(flops=3 * 10**9, bytes_accessed=4 * 10**6, transcendentals=0),
        )(tokens, weights, lengths, cotangent[0])
        return normed[None], gin[None], gw

    placed = (P("dp", "seq", None), P(("seq", "dp"), None), P("dp", None), P("dp", "seq", None))
    return jax.shard_map(
        shards,
        mesh=mesh,
        in_specs=placed,
        out_specs=(P("dp", "seq", None), P("dp", "seq", None), P(("seq", "dp"), None)),
        check_vma=False,
    )
```

time: 119 us -> 105 us (0.88)
  Pallas kernels: 113 us -> 98.7 us
    pallas_call x1, Pallas kernels: 113 us -> 98.7 us  [shards(): pl.pallas_call(functools.partial(kernel, size), out_shape=(jax.ShapeDtype...]
where the time goes in v2:
time: 105 us
  Pallas kernels  98.7 us (94%)
  local copies, waits for them, and re-layouts  5.62 us (5%)
    pallas_call x1, Pallas kernels, shards(): pl.pallas_call(functools.partial(kernel, size), out_shape=(jax.ShapeDtype...  98.7 us
    unnamed x11, local copies, waits for them, and re-layouts  5.62 us

profile of v2, /device:TPU:1, one launch (start us, length us, event | category | flops | bytes accessed | tf_op | source)
XLA Modules:
  0.0 105.0 jit_solution(4200493898221350509)
XLA Ops:
  0.6 0.0 copy-start.3
  0.6 0.6 copy-done.3
  1.3 0.0 copy-start
  1.3 1.2 %copy-done = bf16[1,128,4096]{2,1,0:T(8,128)(2,1)S(1)} copy-done((bf16[1,128,4096]{2,1,0:T(8,128)(2,1)S(1)}, bf16[1,128,4096]{2,1,0:T(8,128)(2,1)}, u32[]{:S(2)}) %copy-start) | copy-done | bytes 1048600
  2.5 0.0 copy-start.1
  2.5 0.8 copy-done.1
  3.4 0.0 copy-start.2
  3.4 0.7 copy-done.2
  4.1 98.7 %shard_map.67 = (bf16[128,256]{1,0:T(8,128)(2,1)S(1)}, bf16[128,4096]{1,0:T(8,128)(2,1)S(1)}, bf16[8,768]{1,0:T(8,128)(2,1)S(1)}) custom-call(bf16[128,4096]{1,0:T(8,128)(2,1)S(1)} %bitcast.6, bf16[8,768]{1,0:T(8,128)(2,1)S(1)} %copy-done.2, s32[1,8]{1,0:T(1,128)S(1)} %copy-done.3, bf16[128,256]{1,0:T(8,128)(2,1)S(1)} %bitcast.7), custom_call_target="tpu_custom_call" | custom-call | flops 3000000000 | bytes 4000000 | tf_op jit(solution)/shard_map/pallas_call | solution.py:613
  102.8 0.6 copy.10
  103.4 1.0 copy.11
  104.4 0.6 copy.12
Async XLA Ops:
  0.6 0.7 copy-start.3
  1.3 1.2 %copy-start = (bf16[1,128,4096]{2,1,0:T(8,128)(2,1)S(1)}, bf16[1,128,4096]{2,1,0:T(8,128)(2,1)}, u32[]{:S(2)}) copy-start(bf16[1,128,4096]{2,1,0:T(8,128)(2,1)} %param.4) | copy-start | bytes 3145732
  2.5 0.8 copy-start.1
  3.4 0.7 copy-start.2

commit v3 on v2

--- a/solution.py
+++ b/solution.py
@@ -28,10 +28,10 @@
     return lax.dot_general(a, b, (((0,), (0,)), ((), ())), preferred_element_type=F32)
 
 
-def kernel(size, tok_hbm, w_hbm, lens_hbm, cot_hbm, normed, gin, gw, *rest):
+def kernel(size, tok_hbm, w_hbm, lens_hbm, cot_hbm, normed_hbm, gin_hbm, gw_hbm, *rest):
     (x2, w, cot, lens, xt, wq, wkv, wsend, wrecv, starts, csend, cots, proj, scan, keep, gbuf, mask, weak, hold, held,
-     kept_n, nsend, nrecv, gown, gsend, grecv, dsend, drecv, load_sem, send_sem, recv_sem) = rest[:31]
-    wg, pg, ring, far, near = (rest[31 + 3 * i : 34 + 3 * i] for i in range(5))
+     kept_n, nsend, nrecv, gown, gsend, grecv, dsend, drecv, normed, gw, load_sem, send_sem, recv_sem) = rest[:33]
+    wg, pg, ring, far, near = (rest[33 + 3 * i : 36 + 3 * i] for i in range(5))
     seqs = 2 * size["z"]
     rows, width = x2.shape[1:]
     chunk = size["y"] * 2 * ROWS
@@ -228,6 +228,7 @@
     second(2)
     masks(0)
     lax.fori_loop(0, seqs, turn(0), 0)
+    query_order = offsets(ORDERS[0][1])
     lists = [(p, sign, gather_hops(p, sign)) for p in (1, 2) for sign in (1, -1)]
     for turn_at in range(max(len(hops) for _, _, hops in lists)):
         for p, sign, hops in lists:
@@ -237,6 +238,11 @@
             arrived(wg[0].at[0, 0, pl.ds(0, size["y"] - 1)], "g1", 0)
         if turn_at % 8 == 3:
             go_round(turn_at // 8)
+        if turn_at % 8 == 5 and turn_at > 8:
+            third = turn_at // 8
+            for o in query_order[2 * third - 1 - (third == 1) : 2 * third + 1]:
+                for sign in (1, -1):
+                    forward(0, sign, 0, o)
         if turn_at == size["y"] - 1:
             swap_x.wait_recv()
         if turn_at >= size["y"]:
@@ -257,13 +263,16 @@
 
     lax.fori_loop(0, seqs, fill, 0)
     swap_c.wait_recv()
-    query_hops = {sign: gather_hops(0, sign) for sign in (1, -1)}
-    early = [hop for hop in query_hops[1] if hop[0] == 0]
-    for k, o in early:
+    query_last = {sign: halves(ORDERS[0][1], sign, query_order) for sign in (1, -1)}
+    for o in query_order[5:-1]:
         for sign in (1, -1):
-            forward(0, sign, k, o)
+            forward(0, sign, 0, o)
+    for o in query_last[1][:-1]:
+        forward(0, 1, 1, o)
     gathered(1)
     gathered(2)
+    for sign in (1, -1):
+        forward(0, sign, 0, query_order[-1])
 
     def tokens_of(zz):
         at_chunk = pl.ds(pl.multiple_of(zz * 2 * chunk, 2 * chunk), 2 * chunk)
@@ -320,9 +329,9 @@
         tail = (mask[b, 2] * block(b, 1).astype(F32)).astype(BF16)
         give(0, b, dot_tn(tail, block(b, 2)))
     send_slices(0, "f1")
-    for sign in (1, -1):
-        for k, o in query_hops[sign][len(early) :]:
-            forward(0, sign, k, o)
+    forward(0, 1, 1, query_last[1][-1])
+    for o in query_last[-1]:
+        forward(0, -1, 1, o)
     take_slices(0, "f1")
     sweep(0, False)
     send_slices(2, "f2")
@@ -517,16 +526,20 @@
     mine, other = kept_n[...].astype(F32), nrecv[...].astype(F32)
     normed[:, :HEAD] = jnp.where(first, mine, other).astype(BF16)
     normed[:, HEAD:] = jnp.where(first, other, mine).astype(BF16)
+    stores = [pltpu.make_async_copy(normed, normed_hbm, load_sem.at[4])]
+    stores[0].start()
     settle_second(1)
     settle_second(2)
     swap_g.wait_recv()
 
     def close(i, _):
         at_chunk = pl.ds(pl.multiple_of(i * chunk, chunk), chunk)
-        gin[:, at_chunk] = (gown[:, at_chunk] + grecv[:, at_chunk].astype(F32)).astype(BF16)
+        grecv[:, at_chunk] = (gown[:, at_chunk] + grecv[:, at_chunk].astype(F32)).astype(BF16)
         return 0
 
     lax.fori_loop(0, seqs, close, 0)
+    stores.append(pltpu.make_async_copy(grecv, gin_hbm, load_sem.at[5]))
+    stores[1].start()
     factor = 1.0 / math.sqrt(size["y"] * 4 * seqs * rows)
     kept = []
     for p, (a1, a2, a3) in enumerate(ORDERS):
@@ -556,7 +569,24 @@
         other = drecv[:, p * HEAD : (p + 1) * HEAD]
         columns += [jnp.where(first, kept[p], other), jnp.where(first, other, kept[p])]
     gw[...] = jnp.concatenate(columns, axis=1).astype(BF16)
+    stores.append(pltpu.make_async_copy(gw, gw_hbm, load_sem.at[6]))
+    stores[2].start()
+    for store in stores:
+        store.wait()
     assert len(names) <= recv_sem.shape[0] and len(sends) <= send_sem.shape[0]
+
+
+def deliver(normed, gin, gw, normed_out, gin_out, gw_out, sem):
+    parts = 4
+    span = gin.shape[0] // parts
+    copies = [pltpu.make_async_copy(normed, normed_out, sem.at[0]), pltpu.make_async_copy(gw, gw_out, sem.at[1])]
+    for i in range(parts):
+        rows = pl.ds(i * span, span)
+        copies.append(pltpu.make_async_copy(gin.at[rows], gin_out.at[rows], sem.at[2 + i]))
+    for copy in copies:
+        copy.start()
+    for copy in copies:
+        copy.wait()
 
 
 def solution(mesh):
@@ -600,31 +630,41 @@
             pltpu.VMEM((rows, width), BF16),
             pltpu.VMEM((8, wide), F32),
             pltpu.VMEM((8, wide), F32),
-            pltpu.SemaphoreType.DMA((4,)),
-            pltpu.SemaphoreType.DMA((40,)),
-            pltpu.SemaphoreType.DMA((352,)),
+            pltpu.VMEM((rows, 2 * HEAD), BF16),
+            pltpu.VMEM((8, 2 * wide), BF16),
+            pltpu.SemaphoreType.DMA((7,)),
+            pltpu.SemaphoreType.DMA((29,)),
+            pltpu.SemaphoreType.DMA((321,)),
         ]
         scratch += [pltpu.VMEM(shape, BF16) for shape in shapes]
         scratch += [pltpu.VMEM(shape, BF16) for shape in shapes]
         scratch += [pltpu.VMEM((2, shape[0] // 2) + shape[1:], BF16) for shape in shapes]
         scratch += [pltpu.VMEM(shape[1:], BF16) for shape in shapes]
         scratch += [pltpu.VMEM(shape[2:], BF16) for shape in shapes]
-        vmem = pl.BlockSpec(memory_space=pltpu.VMEM)
-        normed, gin, gw = pl.pallas_call(
+        hbm = pl.BlockSpec(memory_space=pltpu.HBM)
+        results = (
+            jax.ShapeDtypeStruct((rows, 2 * HEAD), BF16),
+            jax.ShapeDtypeStruct((rows, width), BF16),
+            jax.ShapeDtypeStruct((8, 2 * wide), BF16),
+        )
+        found = pl.pallas_call(
             functools.partial(kernel, size),
-            out_shape=(
-                jax.ShapeDtypeStruct((rows, 2 * HEAD), BF16),
-                jax.ShapeDtypeStruct((rows, width), BF16),
-                jax.ShapeDtypeStruct((8, 2 * wide), BF16),
-            ),
-            in_specs=[pl.BlockSpec(memory_space=pltpu.HBM)] * 4,
-            out_specs=(vmem, vmem, vmem),
+            out_shape=results,
+            in_specs=[hbm] * 4,
+            out_specs=(hbm, hbm, hbm),
             scratch_shapes=scratch,
             compiler_params=pltpu.CompilerParams(
-                collective_id=0, has_side_effects=True, vmem_limit_bytes=48 * 1024 * 1024
+                collective_id=0, has_side_effects=True, vmem_limit_bytes=56 * 1024 * 1024
             ),
             cost_estimate=pl.CostEstimate(flops=3 * 10**9, bytes_accessed=4 * 10**6, transcendentals=0),
         )(tokens, weights, lengths, cotangent[0])
+        normed, gin, gw = pl.pallas_call(
+            deliver,
+            out_shape=results,
+            in_specs=[pl.BlockSpec(memory_space=pltpu.VMEM)] * 3,
+            out_specs=(hbm, hbm, hbm),
+            scratch_shapes=[pltpu.SemaphoreType.DMA((6,))],
+        )(*found)
         return normed[None], gin[None], gw
 
     placed = (P("dp", "seq", None), P(("seq", "dp"), None), P("dp", None), P("dp", "seq", None))

time: 105 us -> 102 us (0.971)
  local copies, waits for them, and re-layouts: 5.62 us -> 0 us
  Pallas kernels: 98.7 us -> 101 us
    unnamed x11 -> x0, local copies, waits for them, and re-layouts: 5.62 us -> none
    pallas_call x1 -> x2, Pallas kernels: 98.7 us -> 101 us  [the longest x1 98.5 us: shards(): pl.pallas_call(functools.partial(kernel, size), out_shape=results, in_spe...]
where the time goes in v3:
time: 102 us; the launch traced here: 101 us
  Pallas kernels  101 us (99%)
    pallas_call x1, Pallas kernels, shards(): pl.pallas_call(functools.partial(kernel, size), out_shape=results, in_spe...  98.5 us
    pallas_call x1, Pallas kernels, shards(): pl.pallas_call(deliver, out_shape=results, in_specs=[pl.BlockSpec(memory_...  2.26 us

profile of v3, /device:TPU:1, one launch (start us, length us, event | category | flops | bytes accessed | tf_op | source)
XLA Modules:
  0.0 101.4 jit_solution(3333007383925122616)
XLA Ops:
  0.6 98.5 %shard_map.67 = (bf16[128,256]{1,0:T(8,128)(2,1)}, bf16[128,4096]{1,0:T(8,128)(2,1)}, bf16[8,768]{1,0:T(8,128)(2,1)}) custom-call(bf16[128,4096]{1,0:T(8,128)(2,1)} %bitcast.4, bf16[8,768]{1,0:T(8,128)(2,1)} %w_hbm.1, s32[1,8]{1,0:T(1,128)} %lens_hbm.1, bf16[128,256]{1,0:T(8,128)(2,1)} %bitcast.6), custom_call_target="tpu_custom_call" | custom-call | flops 3000000000 | bytes 4000000 | tf_op jit(solution)/shard_map/pallas_call | solution.py:650
  99.1 2.3 %shard_map.68 = (bf16[128,256]{1,0:T(8,128)(2,1)}, bf16[128,4096]{1,0:T(8,128)(2,1)}, bf16[8,768]{1,0:T(8,128)(2,1)}) custom-call(bf16[128,256]{1,0:T(8,128)(2,1)} %get-tuple-element.9.normed, bf16[128,4096]{1,0:T(8,128)(2,1)} %get-tuple-element.10.gin, bf16[8,768]{1,0:T(8,128)(2,1)} %get-tuple-element.11.gw), custom_call_target="tpu_custom_call" | custom-call | tf_op jit(solution)/shard_map/pallas_call | solution.py:661

commit v4 on v3

--- a/solution.py
+++ b/solution.py
@@ -419,7 +419,8 @@
         if (p, sign, k - 1, o) in coming:
             coming[p, sign, k - 1, o].wait_recv()
             mine[...] = (mine[...].astype(F32) + slot(p, sign, k - 1, o)[...].astype(F32)).astype(BF16)
-        copy = remote(mine, slot(p, sign, k, o), ("r3", p, sign, k, o), ("r3", p), at(a3, along(a3, sign)))
+        arrival = ("g3", p, -sign, size[a3] // 2 - 1 - k, o) if p == 1 else ("r3", p, sign, k, o)
+        copy = remote(mine, slot(p, sign, k, o), arrival, ("r3", p), at(a3, along(a3, sign)))
         copy.start()
         coming[p, sign, k, o] = copy
 
@@ -507,7 +508,7 @@
         for p, sign, hops in lists:
             if turn_at < len(hops):
                 pass_on(p, sign, *hops[turn_at])
-        upto = min(size["z"], -(-size["z"] * (turn_at + 1) * 4 // (turns * 3)))
+        upto = min(size["z"] // 2, size["z"] * (turn_at + 1) // (turns + 1))
         if upto > done:
             lax.fori_loop(done, upto, inner, 0)
             done = upto
@@ -516,8 +517,6 @@
                 settle(0, o)
         if turn_at % 8 == 1:
             sum_round(turn_at // 8)
-    swap_g = remote(gsend, grecv, ("gi",), ("gi",), sibling)
-    swap_g.start()
     for o in offsets(ORDERS[1][1])[::-1]:
         settle(1, o)
         settle(2, o)
@@ -528,6 +527,9 @@
     normed[:, HEAD:] = jnp.where(first, other, mine).astype(BF16)
     stores = [pltpu.make_async_copy(normed, normed_hbm, load_sem.at[4])]
     stores[0].start()
+    lax.fori_loop(done, size["z"], inner, 0)
+    swap_g = remote(gsend, grecv, ("gi",), ("gi",), sibling)
+    swap_g.start()
     settle_second(1)
     settle_second(2)
     swap_g.wait_recv()
@@ -634,7 +636,7 @@
             pltpu.VMEM((8, 2 * wide), BF16),
             pltpu.SemaphoreType.DMA((7,)),
             pltpu.SemaphoreType.DMA((29,)),
-            pltpu.SemaphoreType.DMA((321,)),
+            pltpu.SemaphoreType.DMA((265,)),
         ]
         scratch += [pltpu.VMEM(shape, BF16) for shape in shapes]
         scratch += [pltpu.VMEM(shape, BF16) for shape in shapes]

time: 102 us -> 101 us (level)
  no operation moved by 1% of the time
where the time goes in v4:
time: 101 us
  Pallas kernels  100 us (99%)
    pallas_call x1, Pallas kernels, shards(): pl.pallas_call(functools.partial(kernel, size), out_shape=results, in_spe...  97.8 us
    pallas_call x1, Pallas kernels, shards(): pl.pallas_call(deliver, out_shape=results, in_specs=[pl.BlockSpec(memory_...  2.26 us

profile of v4, /device:TPU:1, one launch (start us, length us, event | category | flops | bytes accessed | tf_op | source)
XLA Modules:
  0.0 100.7 jit_solution(16296940135597497950)
XLA Ops:
  0.6 97.8 %shard_map.67 = (bf16[128,256]{1,0:T(8,128)(2,1)}, bf16[128,4096]{1,0:T(8,128)(2,1)}, bf16[8,768]{1,0:T(8,128)(2,1)}) custom-call(bf16[128,4096]{1,0:T(8,128)(2,1)} %bitcast.4, bf16[8,768]{1,0:T(8,128)(2,1)} %w_hbm.1, s32[1,8]{1,0:T(1,128)} %lens_hbm.1, bf16[128,256]{1,0:T(8,128)(2,1)} %bitcast.6), custom_call_target="tpu_custom_call" | custom-call | flops 3000000000 | bytes 4000000 | tf_op jit(solution)/shard_map/pallas_call | solution.py:652
  98.4 2.3 %shard_map.68 = (bf16[128,256]{1,0:T(8,128)(2,1)}, bf16[128,4096]{1,0:T(8,128)(2,1)}, bf16[8,768]{1,0:T(8,128)(2,1)}) custom-call(bf16[128,256]{1,0:T(8,128)(2,1)} %get-tuple-element.9.normed, bf16[128,4096]{1,0:T(8,128)(2,1)} %get-tuple-element.10.gin, bf16[8,768]{1,0:T(8,128)(2,1)} %get-tuple-element.11.gw), custom_call_target="tpu_custom_call" | custom-call | tf_op jit(solution)/shard_map/pallas_call | solution.py:663
